TPU v7x, 256 devices: a whole 4x4x8 slice. The times are simulated.
256 devices in a mesh: grp: 8 (over y, core), ctr: 32 (over z, x).
Axes of the slice: x: 4, y: 4, z: 8, core: 2. Of those that a mesh axis runs over, the one named last changes fastest.
Arguments:
- centers: bfloat16 [262144, 1024], P(('grp', 'ctr'))
- coefs: float32 [262144, 1000], P(('grp', 'ctr')), may hold values from -4 to 4
- eigvecs: float32 [65536, 256], P(('grp', 'ctr')), as said below
- eig_weights: float32 [256], replicated, may hold values from 20 to 400
- landmark_index: int32 [65536], P(('grp', 'ctr')), may hold values from 0 to 262143, as said below
- batch_index: int32 [4, 128], replicated, may hold values from 0 to 262143
- targets: float32 [4, 128, 1000], replicated, may hold values from -6 to 6
Outputs:
- new_coefs: float32 [262144, 1000], P(('grp', 'ctr'))
- residuals: float32 [4, 128, 1000], replicated
Inputs may be any that keep to these rules, and one draw needn't show every extreme that they name: `landmark_index`: for every block b of 256 consecutive entries, the entries are distinct centers among b * 1024 to b * 1024 + 1023. `eigvecs`: every column sums to zero over all 65536 landmarks, up to rounding: the eigenvectors are orthogonal to the constant vector.
All inputs are finite; a program needn't handle non-finite values.
Results may differ from a plain program's by a relative error of at most 0.0003.
Values sent between devices are 32-bit elements; how exact they have to be, the bound alone decides.
A program may use at most 128 MiB of HBM per device.

v0:
```python
import jax
import jax.numpy as jnp
from jax import lax
from jax.sharding import PartitionSpec as P

STEPS = 4


floor_sq = 0.01
length_scale = 0.25
step_size = 0.5


def square_norms(rows):
    values = rows.astype(jnp.float32)
    return jnp.sum(values * values, axis=1)


def laplace(left_rows, left_sq, right_rows, right_sq):
    inner = lax.dot_general(
        left_rows, right_rows, (((1,), (1,)), ((), ())), preferred_element_type=jnp.float32
    )
    squared = left_sq[:, None] + right_sq[None, :] - 2.0 * inner
    return jnp.exp(-jnp.sqrt(jnp.maximum(squared, floor_sq)) / length_scale)


def hdot(left_mat, right_mat):
    return jnp.dot(
        left_mat, right_mat, precision=lax.Precision.HIGHEST, preferred_element_type=jnp.float32
    )


def tdot(left_mat, right_mat):
    return lax.dot_general(
        left_mat,
        right_mat,
        (((0,), (0,)), ((), ())),
        precision=lax.Precision.HIGHEST,
        preferred_element_type=jnp.float32,
    )


def body(centers, coefs, eigvecs, eig_weights, landmark_index, batch_index, targets):
    center_count = centers.shape[0]
    offset = lax.axis_index(("grp", "ctr")) * center_count
    center_sq = square_norms(centers)
    local_batch = batch_index - offset
    is_owned = (local_batch >= 0) & (local_batch < center_count)
    safe_rows = jnp.clip(local_batch, 0, center_count - 1)
    picked = jnp.where(is_owned[:, :, None], centers[safe_rows].astype(jnp.float32), 0.0)
    arrived = lax.psum(picked, ("grp", "ctr"))
    batch_sq_all = jnp.sum(arrived * arrived, axis=2)
    all_batches = arrived.astype(jnp.bfloat16)
    land_local = landmark_index - offset
    landmark_rows = centers[land_local]
    landmark_sq = center_sq[land_local]
    coeffs = coefs
    collected = []
    for iteration in range(STEPS):
        batch_rows = all_batches[iteration]
        batch_sq = batch_sq_all[iteration]
        kernel = laplace(batch_rows, batch_sq, centers, center_sq)
        land_kernel = laplace(landmark_rows, landmark_sq, batch_rows, batch_sq)
        predicted = lax.psum(hdot(kernel, coeffs), ("grp", "ctr"))
        residual = predicted - targets[iteration]
        projected = lax.psum(tdot(eigvecs, hdot(land_kernel, residual)), ("grp", "ctr"))
        correction = hdot(eigvecs, eig_weights[:, None] * projected)
        batch_update = jnp.where(is_owned[iteration][:, None], -step_size * residual, 0.0)
        coeffs = (
            coeffs.at[safe_rows[iteration]]
            .add(batch_update)
            .at[land_local]
            .add(step_size * correction)
        )
        collected.append(residual)
    return (coeffs, jnp.stack(collected))


def solution(mesh):
    in_specs = (
        P(("grp", "ctr"), None),
        P(("grp", "ctr"), None),
        P(("grp", "ctr"), None),
        P(),
        P(("grp", "ctr")),
        P(),
        P(),
    )
    out_specs = (P(("grp", "ctr"), None), P())
    return jax.shard_map(body, mesh=mesh, in_specs=in_specs, out_specs=out_specs, check_vma=False)
```

profile of v0, /device:TPU:1, one launch (start us, length us, event | category | flops | bytes accessed | tf_op | source)
XLA Modules:
  0.0 2422.8 jit_solution(13453031705019621363)
XLA Ops:
  8.6 4.6 gather_fusion
  13.3 1.5 convert_select_fusion
  16.6 262.0 %all-reduce.10.cloned.1.call-done = f32[4,128,1024]{2,1,0:T(8,128)} async-done(((f32[4,128,1024]{2,1,0:T(8,128)}), f32[4,128,1024]{2,1,0:T(8,128)}) %all-reduce.10.cloned.1.call-update) | async-done | bytes 2097168 | tf_op jit(solution)/shard_map/psum | solution.py:51
  278.5 2.7 fusion.73
  282.9 4.1 fusion.74
  287.1 1.9 gather_fusion.1
  289.1 2.0 gather_fusion.2
  291.1 5.3 copy.15
  297.8 240.4 %all-reduce.12.cloned.1.call-done = f32[128,1000]{0,1:T(8,128)} async-done(((f32[128,1000]{0,1:T(8,128)}), f32[128,1000]{0,1:T(8,128)}) %all-reduce.12.cloned.1.call-update) | async-done | bytes 512016 | tf_op jit(solution)/shard_map/psum | solution.py:64
  538.2 2.2 fusion.66
  540.4 2.1 convolution_bitcast_fusion.3
  542.8 2.8 fusion.21
  545.5 2.0 fusion.65
  547.7 5.7 scatter_fusion
  553.4 245.5 %all-reduce.14.cloned.1.call-done = f32[256,1000]{1,0:T(8,128)} async-done(((f32[256,1000]{1,0:T(8,128)}), f32[256,1000]{1,0:T(8,128)}) %all-reduce.14.cloned.1.call-update) | async-done | bytes 1024016 | tf_op jit(solution)/shard_map/psum | solution.py:66
  798.9 4.1 fusion.3
  802.9 1.5 copy.17
  804.5 6.7 scatter_fusion.1
  811.2 9.8 fusion.75
  822.8 249.4 %all-reduce.16.cloned.1.call-done = f32[128,1000]{0,1:T(8,128)} async-done(((f32[128,1000]{0,1:T(8,128)}), f32[128,1000]{0,1:T(8,128)}) %all-reduce.16.cloned.1.call-update) | async-done | bytes 512016 | tf_op jit(solution)/shard_map/psum | solution.py:64
  1072.2 2.2 fusion.68
  1074.4 2.1 convolution_bitcast_fusion.2
  1076.5 2.8 fusion.15
  1079.3 2.0 fusion.67
  1081.5 5.7 scatter_fusion.2
  1087.2 246.3 %all-reduce.18.cloned.1.call-done = f32[256,1000]{1,0:T(8,128)} async-done(((f32[256,1000]{1,0:T(8,128)}), f32[256,1000]{1,0:T(8,128)}) %all-reduce.18.cloned.1.call-update) | async-done | bytes 1024016 | tf_op jit(solution)/shard_map/psum | solution.py:66
  1333.5 4.1 fusion.2
  1337.6 1.5 copy.19
  1339.1 6.8 scatter_fusion.3
  1346.0 9.8 fusion.76
  1357.2 249.7 %all-reduce.20.cloned.1.call-done = f32[128,1000]{0,1:T(8,128)} async-done(((f32[128,1000]{0,1:T(8,128)}), f32[128,1000]{0,1:T(8,128)}) %all-reduce.20.cloned.1.call-update) | async-done | bytes 512016 | tf_op jit(solution)/shard_map/psum | solution.py:64
  1606.9 2.2 fusion.70
  1609.1 2.1 convolution_bitcast_fusion.1
  1611.3 2.8 fusion.9
  1615.4 5.9 scatter_fusion.4
  1621.3 246.2 %all-reduce.22.cloned.1.call-done = f32[256,1000]{1,0:T(8,128)} async-done(((f32[256,1000]{1,0:T(8,128)}), f32[256,1000]{1,0:T(8,128)}) %all-reduce.22.cloned.1.call-update) | async-done | bytes 1024016 | tf_op jit(solution)/shard_map/psum | solution.py:66
  1867.6 3.1 fusion.1
  1871.0 6.7 scatter_fusion.5
  1877.7 9.9 fusion.77
  1889.3 249.5 %all-reduce.24.cloned.1.call-done = f32[128,1000]{0,1:T(8,128)} async-done(((f32[128,1000]{0,1:T(8,128)}), f32[128,1000]{0,1:T(8,128)}) %all-reduce.24.cloned.1.call-update) | async-done | bytes 512016 | tf_op jit(solution)/shard_map/psum | solution.py:64
  2138.8 2.0 fusion.72
  2140.8 2.1 convolution_bitcast_fusion
  2142.9 1.9 fusion.71
  2146.1 5.8 scatter_fusion.6
  2153.3 247.0 %all-reduce.26.cloned.1.call-done = f32[256,1000]{1,0:T(8,128)} async-done(((f32[256,1000]{1,0:T(8,128)}), f32[256,1000]{1,0:T(8,128)}) %all-reduce.26.cloned.1.call-update) | async-done | bytes 1024016 | tf_op jit(solution)/shard_map/psum | solution.py:66
  2400.3 3.1 fusion
  2403.8 6.7 scatter_fusion.7
  2410.5 5.3 copy.24
  (96 shorter events, 16.5 us)
Async XLA Ops:
  7.2 533.2 %copy-start = (f32[256,256]{1,0:T(8,128)S(1)}, f32[256,256]{1,0:T(8,128)}, u32[]{:S(2)}) copy-start(f32[256,256]{1,0:T(8,128)} %param.9) | copy-start | bytes 786436
  7.2 271.4 %all-reduce.10.cloned.1.call-start = ((), (), s32[]{:S(2)}) async-start(), calls=%async_computation | async-start | bytes 4194304 | tf_op jit(solution)/shard_map/psum | solution.py:51
  13.2 1.6 copy-start.20
  13.3 2.8 copy-start.1
  14.8 523.3 %all-reduce.12.cloned.1.call-start = ((), (), s32[]{:S(2)}) async-start(), calls=%async_computation.1 | async-start | bytes 1024000 | tf_op jit(solution)/shard_map/psum | solution.py:64
  278.5 4.4 copy-start.2
  281.2 15.2 copy-start.9
  281.9 5.2 copy-start.27
  287.1 511.8 %all-reduce.14.cloned.1.call-start = ((), (), s32[]{:S(2)}) async-start(), calls=%async_computation.2 | async-start | bytes 2097152 | tf_op jit(solution)/shard_map/psum | solution.py:66
  540.4 2.4 copy-start.26
  542.5 3.1 copy-start.6
  542.5 3.1 copy-start.18
  542.5 529.7 %all-reduce.16.cloned.1.call-start = ((), (), s32[]{:S(2)}) async-start(), calls=%async_computation.3 | async-start | bytes 1024000 | tf_op jit(solution)/shard_map/psum | solution.py:64
  545.5 2.2 copy-start.19
  547.7 251.2 %copy-start.13 = (f32[256]{0:T(256)S(1)}, f32[256]{0:T(256)}, u32[]{:S(2)}) copy-start(f32[256]{0:T(256)} %param.10) | copy-start | bytes 3076
  811.2 10.3 copy-start.10
  811.2 10.3 copy-start.21
  821.1 512.5 %all-reduce.18.cloned.1.call-start = ((), (), s32[]{:S(2)}) async-start(), calls=%async_computation.4 | async-start | bytes 2097152 | tf_op jit(solution)/shard_map/psum | solution.py:66
  1074.4 2.2 copy-start.25
  1076.5 2.9 copy-start.8
  1076.5 2.9 copy-start.16
  1076.5 530.4 %all-reduce.20.cloned.1.call-start = ((), (), s32[]{:S(2)}) async-start(), calls=%async_computation.5 | async-start | bytes 1024000 | tf_op jit(solution)/shard_map/psum | solution.py:64
  1079.3 2.2 copy-start.17
  1346.0 9.9 copy-start.11
  1355.9 511.7 %all-reduce.22.cloned.1.call-start = ((), (), s32[]{:S(2)}) async-start(), calls=%async_computation.6 | async-start | bytes 2097152 | tf_op jit(solution)/shard_map/psum | solution.py:66
  1609.1 2.2 copy-start.23
  1611.2 2.9 copy-start.7
  1611.2 2.9 copy-start.14
  1611.2 527.5 %all-reduce.24.cloned.1.call-start = ((), (), s32[]{:S(2)}) async-start(), calls=%async_computation.7 | async-start | bytes 1024000 | tf_op jit(solution)/shard_map/psum | solution.py:64
  1614.1 1.3 copy-start.15
  1877.7 10.3 copy-start.12
  1877.7 10.3 copy-start.22
  1877.7 10.3 copy-start.24
  1877.7 261.1 %copy-start.3 = (f32[4,128,1000]{1,2,0:T(8,128)S(1)}, f32[4,128,1000]{1,2,0:T(8,128)}, u32[]{:S(2)}) copy-start(f32[4,128,1000]{1,2,0:T(8,128)} %param.13) | copy-start | bytes 6144004
  1887.7 512.6 %all-reduce.26.cloned.1.call-start = ((), (), s32[]{:S(2)}) async-start(), calls=%async_computation.8 | async-start | bytes 2097152 | tf_op jit(solution)/shard_map/psum | solution.py:66
  2146.1 5.8 copy-start.4
  2146.1 5.8 copy-start.5
Sparse Core Ops, SparseCore 0:
  15.0 263.5 all-reduce.9
  287.2 250.9 all-reduce.11
  544.2 254.6 all-reduce.13
  821.2 250.9 all-reduce.15
  1078.9 254.5 all-reduce.17
  1356.0 250.9 all-reduce.19
  1612.9 254.5 all-reduce.21
  1887.8 250.9 all-reduce.23
  2145.7 254.6 all-reduce.25
where the time goes:
time: 2430 us; the launch traced here: 2420 us
  waiting for transfers between devices  2240 us (92%)
  matrix products  79.5 us (3%)
  other arithmetic  65.1 us (3%)
  local copies, waits for them, and re-layouts  26.1 us (1%)
    psum x4, waiting for transfers between devices, body(): predicted = lax.psum(hdot(kernel, coeffs), ('grp', 'ctr'))  989 us
    psum x4, waiting for transfers between devices, body(): lax.psum(tdot(eigvecs, hdot(land_kernel, residual)), ('grp', 'ctr'))  985 us
    psum x1, waiting for transfers between devices, body(): arrived = lax.psum(picked, ('grp', 'ctr'))  262 us
    dot_general x12, matrix products, hdot(): jnp.dot(left_mat, right_mat, precision=lax.Precision.HIGHEST, preferred_e...  56.6 us
    scatter-add x8, other arithmetic, body(): coeffs = coeffs.at[safe_rows[iteration]].add(batch_update).at[land_local]...  49.9 us
  transfers between devices with their start and end apart: 9, of which 9 were waited for; matrix products, arithmetic and copies ran while one was open for 2% of the time, Pallas kernels for 0%

commit v1 on v0

v1 whole, which is shorter than its diff:
```python
import functools

import jax
import jax.numpy as jnp
from jax import lax
from jax.experimental import pallas as pl
from jax.experimental.pallas import tpu as pltpu
from jax.sharding import PartitionSpec as P

STEPS = 4
BATCH = 128
EIGS = 256
LANES = 128
SIZES = {"x": 4, "y": 4, "z": 8}

floor_sq = 0.01
length_scale = 0.25
step_size = 0.5

MESH = pl.DeviceIdType.MESH


def allreduce_kernel(sizes, owners, orders, shapes, a_ref, o_ref, *scratch):
    parts = len(owners)
    send, recv = scratch[-2:]
    bufs = scratch[:-2]
    grp, ctr = lax.axis_index("grp"), lax.axis_index("ctr")
    core, y = lax.rem(grp, 2), lax.div(grp, 2)
    z, x = lax.div(ctr, sizes["x"]), lax.rem(ctr, sizes["x"])
    me = {"x": x, "y": y, "z": z}

    def shifted(axis, by):
        return lax.rem(me[axis] + by, sizes[axis])

    def device(axis, by):
        if axis == "c":
            return (y * 2 + 1 - core, ctr)
        to = shifted(axis, by)
        if axis == "x":
            return (grp, z * sizes["x"] + to)
        if axis == "y":
            return (to * 2 + core, ctr)
        return (grp, to * sizes["x"] + x)

    peers = [("c", 1)] + [(axis, by) for axis in "xyz" for by in range(1, sizes[axis])]
    barrier = pltpu.get_barrier_semaphore()
    for axis, by in peers:
        pl.semaphore_signal(barrier, inc=1, device_id=device(axis, by), device_id_type=MESH)
    pl.semaphore_wait(barrier, len(peers))

    count = [0] * parts

    def remote(part, src, dst, to):
        index = count[part]
        count[part] += 1
        return pltpu.make_async_remote_copy(
            src_ref=src,
            dst_ref=dst,
            send_sem=send.at[part, index],
            recv_sem=recv.at[part, index],
            device_id=to,
            device_id_type=MESH,
        )

    def along(ref, dims, axis, index):
        if axis == "z":
            columns = pl.ds(pl.multiple_of(index * LANES, LANES), LANES)
            return ref.at[(slice(None),) * (len(dims) + 1) + (columns,)]
        return ref.at[tuple(index if dim == axis else slice(None) for dim in dims)]

    def region(part, fixed):
        columns = slice(None)
        if "z" in fixed:
            columns = pl.ds(pl.multiple_of(z * LANES, LANES), LANES)
        return o_ref.at[
            part, x if "x" in fixed else slice(None), y if "y" in fixed else slice(None), :, columns
        ]

    every = []

    def mine(part):
        return core == owners[part]

    state = []
    for part in range(parts):
        taken = bufs[8 * part]
        copy = remote(part, a_ref.at[part], taken, device("c", 1))
        pl.when(jnp.logical_not(mine(part)))(copy.start)
        state.append(([copy], a_ref.at[part], [taken], "xy"))

    for phase in range(4):
        nexts = []
        for part in range(parts):
            copies, own, arrived, dims = state[part]
            total = bufs[8 * part + 2 * phase + 1] if phase < 3 else region(part, "xyz")
            sends = []
            if phase < 3:
                axis = orders[part][phase]
                landing = bufs[8 * part + 2 * phase + 2]
                for by in range(1, sizes[axis]):
                    sends.append(
                        remote(
                            part,
                            along(total, dims, axis, shifted(axis, by)),
                            landing.at[by - 1],
                            device(axis, by),
                        )
                    )
                after = dims.replace(axis, "")
                nexts.append(
                    (
                        sends,
                        along(total, dims, axis, me[axis]),
                        [landing.at[by - 1] for by in range(1, sizes[axis])],
                        after,
                    )
                )
            else:
                axis = orders[part][2]
                for by in range(1, sizes[axis]):
                    here = region(part, "xyz")
                    sends.append(remote(part, here, here, device(axis, by)))
                nexts.append((sends, None, None, None))

            @pl.when(mine(part))
            def _(copies=copies, own=own, arrived=arrived, total=total, sends=sends):
                for copy in copies:
                    copy.wait_recv()
                value = own[...]
                for ref in arrived:
                    value = value + ref[...]
                total[...] = value
                for copy in sends:
                    copy.start()

            every.append((part, phase == 0, copies))
        state = nexts

    for phase in range(3):
        nexts = []
        for part in range(parts):
            copies = state[part][0]
            order = orders[part]
            here = region(part, order[: 2 - phase])
            sends = []
            if phase < 2:
                axis = order[1 - phase]
                for by in range(1, sizes[axis]):
                    sends.append(remote(part, here, here, device(axis, by)))
            else:
                sends.append(remote(part, here, here, device("c", 1)))
            nexts.append((sends, None, None, None))

            @pl.when(mine(part))
            def _(copies=copies, sends=sends):
                for copy in copies:
                    copy.wait_recv()
                for copy in sends:
                    copy.start()

            every.append((part, False, copies))
        state = nexts
    for part in range(parts):
        pl.when(jnp.logical_not(mine(part)))(state[part][0][0].wait_recv)
        every.append((part, False, state[part][0]))

    for part, others, copies in every:
        condition = jnp.logical_not(mine(part)) if others else mine(part)

        @pl.when(condition)
        def _(copies=copies):
            for copy in copies:
                copy.wait_send()


def allreduce(a, owners, orders, sizes, collective_id):
    scratch = []
    copies = 2 + 2 * sum(size - 1 for size in sizes.values())
    for order in orders:
        block = list(a.shape[1:])
        dims = "xy"
        scratch += [pltpu.VMEM(tuple(block), a.dtype)] * 2
        for phase, axis in enumerate(order):
            if axis == "z":
                block[-1] = LANES
            else:
                block.pop(dims.index(axis))
                dims = dims.replace(axis, "")
            scratch.append(pltpu.VMEM((sizes[axis] - 1,) + tuple(block), a.dtype))
            if phase < 2:
                scratch.append(pltpu.VMEM(tuple(block), a.dtype))
        scratch.append(pltpu.VMEM((8, LANES), a.dtype))
    scratch += [pltpu.SemaphoreType.DMA((len(owners), copies))] * 2
    return pl.pallas_call(
        functools.partial(allreduce_kernel, sizes, owners, orders, None),
        out_shape=jax.ShapeDtypeStruct(a.shape, a.dtype),
        in_specs=[pl.BlockSpec(memory_space=pltpu.VMEM)],
        out_specs=pl.BlockSpec(memory_space=pltpu.VMEM),
        scratch_shapes=scratch,
        compiler_params=pltpu.CompilerParams(
            collective_id=collective_id, has_side_effects=True, vmem_limit_bytes=40 * 2**20
        ),
    )(a)


def laplace(left_rows, left_sq, right_rows, right_sq):
    inner = lax.dot_general(
        left_rows, right_rows, (((1,), (1,)), ((), ())), preferred_element_type=jnp.float32
    )
    squared = left_sq[:, None] + right_sq[None, :] - 2.0 * inner
    return jnp.exp(-jnp.sqrt(jnp.maximum(squared, floor_sq)) / length_scale)


def fdot(left, right, dims=((1,), (0,)), precision=lax.Precision.HIGH):
    return lax.dot_general(
        left, right, (dims, ((), ())), precision=precision, preferred_element_type=jnp.float32
    )


def body(sizes, centers, coefs, eigvecs, eig_weights, landmark_index, batch_index, targets):
    count, width = centers.shape
    outputs = coefs.shape[1]
    tall = sizes["x"] * sizes["y"] * 8
    total = STEPS * BATCH
    offset = lax.axis_index(("grp", "ctr")) * count
    places = lax.broadcasted_iota(jnp.int32, (1, count), 1)

    owned = (batch_index.reshape(total, 1) - offset) == places
    picked = jnp.dot(
        owned.astype(jnp.bfloat16), centers, preferred_element_type=jnp.float32
    )
    parts = total // tall
    shape = (parts, sizes["x"], sizes["y"], 8, width)
    owners = tuple(p // (parts // 2) for p in range(parts))
    orders = tuple(("xyz", "yxz")[p % 2] for p in range(parts))
    arrived = allreduce(picked.reshape(shape), owners, orders, sizes, 0).reshape(total, width)

    batch_sq = jnp.sum(arrived * arrived, axis=1)
    batch = arrived.astype(jnp.bfloat16)
    values = centers.astype(jnp.float32)
    center_sq = jnp.sum(values * values, axis=1)
    kernel = laplace(batch, batch_sq, centers, center_sq)
    between = laplace(batch, batch_sq, batch, batch_sq)

    at_landmark = (landmark_index.reshape(-1, 1) - offset) == places
    spread = fdot(at_landmark.astype(jnp.float32), eigvecs, ((0,), (0,)), lax.Precision.HIGHEST)

    predicted = jnp.pad(fdot(kernel, coefs), ((0, 0), (0, width - outputs)))
    gradient = fdot(kernel, spread)
    across = width // EIGS
    gradient = gradient.reshape(across, total // across, EIGS).transpose(1, 0, 2)
    extra = gradient.reshape(total // across, width)
    packed = jnp.concatenate([predicted, extra], axis=0)
    parts = packed.shape[0] // tall
    shape = (parts, sizes["x"], sizes["y"], 8, width)
    more = extra.shape[0] // tall
    owners = owners + (0,) * more
    orders = orders + ("zxy",) * more
    summed = allreduce(packed.reshape(shape), owners, orders, sizes, 1).reshape(packed.shape)

    predicted = summed[:total, :outputs]
    gradient = summed[total:].reshape(total // across, across, EIGS).transpose(1, 0, 2)
    gradient = gradient.reshape(total, EIGS)
    weighted = gradient * (step_size * eig_weights)[None, :]
    effect = fdot(weighted, gradient, ((1,), (1,))) - step_size * between
    residuals = []
    for step in range(STEPS):
        rows = slice(step * BATCH, (step + 1) * BATCH)
        residual = predicted[rows] - targets[step]
        if step > 0:
            residual = residual + fdot(
                effect[rows, : step * BATCH],
                jnp.concatenate(residuals, axis=0),
                precision=lax.Precision.HIGHEST,
            )
        residuals.append(residual)
    residual = jnp.concatenate(residuals, axis=0)
    update = fdot(spread, weighted, ((1,), (1,))) - step_size * owned.T.astype(jnp.float32)
    return coefs + fdot(update, residual), residual.reshape(STEPS, BATCH, outputs)


def solution(mesh, sizes=SIZES):
    in_specs = (
        P(("grp", "ctr"), None),
        P(("grp", "ctr"), None),
        P(("grp", "ctr"), None),
        P(),
        P(("grp", "ctr")),
        P(),
        P(),
    )
    out_specs = (P(("grp", "ctr"), None), P())
    return jax.shard_map(
        functools.partial(body, sizes),
        mesh=mesh,
        in_specs=in_specs,
        out_specs=out_specs,
        check_vma=False,
    )
```

time: 2430 us -> 150 us (0.06)
  waiting for transfers between devices: 2240 us -> 0 us
  Pallas kernels: 0 us -> 96.4 us
  other arithmetic: 65.1 us -> 10.2 us
  matrix products: 79.5 us -> 30.1 us
    psum x9 -> x0, waiting for transfers between devices: 2240 us -> none  [the longest x4 989 us: body(): predicted = lax.psum(hdot(kernel, coeffs), ('grp', 'ctr'))]
    pallas_call x0 -> x2, Pallas kernels: none -> 96.4 us  [allreduce(): pl.pallas_call(functools.partial(allreduce_kernel, sizes, owners, orders,...]
    scatter-add x8 -> x0, other arithmetic: 49.9 us -> none  [body(): coeffs = coeffs.at[safe_rows[iteration]].add(batch_update).at[land_local]...]
    dot_general x16 -> x10, matrix products: 65 us -> 24.4 us  [the longest x9 23.1 us: fdot(): lax.dot_general(left, right, (dims, ((), ())), precision=precision, prefe...]
  transfers between devices with their start and end apart: 9 -> 0, of which waited for: 9 -> 0; matrix products, arithmetic and copies ran while one was open for 2% -> 0% of each run, Pallas kernels for 0% -> 0%
where the time goes in v1:
time: 150 us; the launch traced here: 149 us
  Pallas kernels  96.4 us (64%)
  matrix products  30.1 us (20%)
  local copies, waits for them, and re-layouts  11.5 us (8%)
  other arithmetic  10.2 us (7%)
    pallas_call x2, Pallas kernels, allreduce(): pl.pallas_call(functools.partial(allreduce_kernel, sizes, owners, orders,...  96.4 us
    dot_general x9, matrix products, fdot(): lax.dot_general(left, right, (dims, ((), ())), precision=precision, prefe...  23.1 us
    dot_general x2, matrix products, laplace(): lax.dot_general(left_rows, right_rows, (((1,), (1,)), ((), ())), preferre...  5.76 us
    unnamed x28, local copies, waits for them, and re-layouts  5.69 us

profile of v1, /device:TPU:1, one launch (start us, length us, event | category | flops | bytes accessed | tf_op | source)
XLA Modules:
  0.0 149.1 jit_solution(4312138809208083408)
XLA Ops:
  0.6 0.0 copy-start
  0.6 0.0 copy-start.7
  0.7 0.8 broadcast_multiply_fusion
  1.5 0.7 broadcast_subtract_fusion
  2.2 0.7 subtract_bitcast_fusion
  2.9 2.1 %multiply_reduce_fusion = f32[1024]{0:T(1024)S(1)} fusion(bf16[1024,1024]{1,0:T(8,128)(2,1)} %param.7), kind=kLoop, calls=%fused_computation | loop fusion | flops 3144704 | bytes 2101248 | tf_op jit(solution)/shard_map/reduce_sum | solution.py:241
  4.9 0.0 copy-done
  4.9 1.1 fusion.24
  6.0 0.0 copy-done.7
  6.0 0.0 copy-start.5
  6.1 1.3 fusion.2
  7.4 49.8 %shard_map.86 = f32[4,4,4,8,1024]{4,3,2,1,0:T(8,128)S(1)} custom-call(f32[4,4,4,8,1024]{4,3,2,1,0:T(8,128)S(1)} %bitcast.52), custom_call_target="tpu_custom_call" | custom-call | tf_op jit(solution)/shard_map/pallas_call | solution.py:194
  57.2 1.3 multiply_reduce_fusion.1
  58.4 0.1 add.46
  58.5 0.0 copy-start.11
  58.5 3.8 %fusion.15 = f32[512,512]{1,0:T(8,128)} fusion(bf16[512,1024]{1,0:T(8,128)(2,1)} %bitcast.58, f32[512]{0:T(512)S(1)} %add.46), kind=kOutput, calls=%fused_computation.27 | convolution fusion | flops 538705920 | bytes 2099200 | tf_op jit(solution)/shard_map/dot_general | solution.py:207
  62.3 2.0 %multiply_exponential_fusion = f32[512,1024]{1,0:T(8,128)S(1)} fusion(bf16[512,1024]{1,0:T(8,128)(2,1)S(1)} %bitcast.59, bf16[1024,1024]{1,0:T(8,128)(2,1)S(1)} %copy-done.7, f32[1024]{0:T(1024)S(1)} %multiply_reduce_fusion, f32[512]{0:T(512)S(1)} %add.46), kind=kOutput, calls=%fused_computation.7 | convolution fusion | flops 1076887552 | bytes 5249024 | tf_op jit(solution)/shard_map/dot_general | solution.py:207
  64.3 1.0 fusion.42
  65.4 0.0 copy-done.2
  65.4 4.8 %fusion.41 = f32[512,1000]{0,1:T(8,128)} fusion(f32[512,1024]{1,0:T(8,128)S(1)} %multiply_exponential_fusion, f32[1024,1000]{0,1:T(8,128)S(1)} %copy-done.2), kind=kOutput, calls=%fused_computation.62 | convolution fusion | flops 3145728000 | bytes 8241152 | tf_op jit(solution)/shard_map/dot_general | solution.py:215
  70.1 0.2 copy.16
  70.3 1.8 %select_maximum_fusion = f32[640,1024]{0,1:T(8,128)S(1)} fusion(f32[512,1000]{0,1:T(8,128)} %fusion.41, f32[128,1024]{0,1:T(8,128)S(1)} %bitcast.56), kind=kLoop, calls=%fused_computation.1 | loop fusion | flops 1966080 | bytes 5193728 | tf_op jit(solution)/shard_map/concatenate | solution.py:253
  72.1 2.1 %copy.17 = f32[640,1024]{1,0:T(8,128)} copy(f32[640,1024]{0,1:T(8,128)S(1)} %select_maximum_fusion) | data formatting | bytes 5242880 | tf_op jit(solution)/shard_map/concatenate | solution.py:253
  74.2 1.7 %copy-done.1 = f32[640,1024]{1,0:T(8,128)S(1)} copy-done((f32[640,1024]{1,0:T(8,128)S(1)}, f32[640,1024]{1,0:T(8,128)}, u32[]{:S(2)}) %copy-start.1) | copy-done | bytes 2621464
  75.9 46.6 %shard_map.87 = f32[5,4,4,8,1024]{4,3,2,1,0:T(8,128)S(1)} custom-call(f32[5,4,4,8,1024]{4,3,2,1,0:T(8,128)S(1)} %bitcast.51), custom_call_target="tpu_custom_call" | custom-call | tf_op jit(solution)/shard_map/pallas_call | solution.py:194
  122.6 0.8 slice.42
  123.4 1.3 reshape.63
  124.7 0.0 copy-start.10
  124.7 0.1 bitcast_multiply_fusion
  124.8 0.1 copy.18
  124.9 1.0 copy-done.10
  125.9 1.6 %convolution_subtract_fusion = f32[512,512]{1,0:T(8,128)} fusion(f32[512,512]{1,0:T(8,128)S(1)} %copy-done.10, f32[512,256]{1,0:T(8,128)S(1)} %bitcast.57, f32[512,256]{1,0:T(8,128)S(1)} %bitcast.53), kind=kOutput, calls=%fused_computation.21 | convolution fusion | flops 402915328 | bytes 3145728 | tf_op jit(solution)/shard_map/dot_general | solution.py:215
  127.5 2.3 %fusion.28 = f32[1024,512]{1,0:T(8,128)} fusion(f32[1024,256]{1,0:T(8,128)S(1)} %copy-done.6, f32[512,256]{1,0:T(8,128)S(1)} %bitcast.54, f32[256]{0:T(256)S(1)} %broadcast_multiply_fusion), kind=kOutput, calls=%fused_computation.42 | convolution fusion | flops 805437440 | bytes 3671040 | tf_op jit(solution)/shard_map/dot_general | solution.py:215
  129.8 1.2 fusion.40
  131.0 1.3 copy.27
  132.3 1.2 copy.26
  133.6 0.0 copy-done.8
  133.6 0.2 copy.25
  133.8 0.2 copy.24
  134.0 0.0 copy-start.9
  134.0 1.2 bitcast_subtract_fusion.3
  135.2 0.0 copy-start.4
  135.2 2.2 %convolution_add_fusion.2 = f32[128,1000]{0,1:T(8,128)S(1)} fusion(f32[128,1000]{0,1:T(8,128)S(1)} %bitcast_subtract_fusion.3, f32[128,1000]{0,1:T(8,128)S(1)} %copy.25, f32[4,128,1000]{1,2,0:T(8,128)} %param.13, f32[512,512]{1,0:T(8,128)} %convolution_subtract_fusion), kind=kOutput, calls=%fused_computation.30 | convolution fusion | flops 196864000 | bytes 2113536 | tf_op jit(solution)/shard_map/dot_general | solution.py:215
  137.5 0.0 copy-start.3
  137.5 2.0 %convolution_add_fusion.1 = f32[128,1000]{0,1:T(8,128)S(1)} fusion(f32[128,1000]{0,1:T(8,128)S(1)} %convolution_add_fusion.2, f32[128,1000]{0,1:T(8,128)S(1)} %bitcast_subtract_fusion.3, f32[128,1000]{0,1:T(8,128)S(1)} %copy.26, f32[4,128,1000]{1,2,0:T(8,128)S(1)} %copy-done.9, f32[512,512]{1,0:T(8,128)} %convolution_subtract_fusion), kind=kOutput, calls=%fused_computation.29 | convolution fusion | flops 393728000 | bytes 2691072 | tf_op jit(solution)/shard_map/dot_general | solution.py:215
  139.5 2.7 %fusion.16 = f32[128,1000]{0,1:T(8,128)S(1)} fusion(f32[128,1000]{0,1:T(8,128)S(1)} %convolution_add_fusion.1, f32[128,1000]{0,1:T(8,128)S(1)} %convolution_add_fusion.2, f32[128,1000]{0,1:T(8,128)S(1)} %bitcast_subtract_fusion.3, f32[128,1000]{0,1:T(8,128)S(1)} %copy.27, f32[4,128,1000]{1,2,0:T(8,128)S(1)} %copy-done.9, ...), kind=kOutput, calls=%fused_computation.28 | convolution fusion | flops 590848000 | bytes 3268608 | tf_op jit(solution)/shard_map/dot_general | solution.py:215
  142.2 5.3 %convolution_add_fusion = f32[1024,1000]{0,1:T(8,128)} fusion(f32[1024,1000]{0,1:T(8,128)S(1)} %copy-done.3, f32[1024,512]{1,0:T(8,128)S(1)} %copy-done.4, f32[128,1000]{0,1:T(8,128)S(1)} %fusion.16, f32[128,1000]{0,1:T(8,128)S(1)} %convolution_add_fusion.1, f32[128,1000]{0,1:T(8,128)S(1)} %convolution_add_fusion.2, ...), kind=kOutput, calls=%fused_computation.3 | convolution fusion | flops 3149860864 | bytes 12339200 | tf_op jit(solution)/shard_map/dot_general | solution.py:215
  147.6 1.5 %copy_bitcast_fusion = f32[4,128,1000]{1,2,0:T(8,128)} fusion(f32[128,1000]{0,1:T(8,128)S(1)} %fusion.16, f32[128,1000]{0,1:T(8,128)S(1)} %convolution_add_fusion.1, f32[128,1000]{0,1:T(8,128)S(1)} %convolution_add_fusion.2, f32[128,1000]{0,1:T(8,128)S(1)} %bitcast_subtract_fusion.3), kind=kLoop, calls=%fused_computation.11 | loop fusion | flops 1536000 | bytes 4096000
  (10 shorter events, 0.0 us)
Async XLA Ops:
  0.6 4.3 %copy-start = (f32[256,256]{1,0:T(8,128)S(1)}, f32[256,256]{1,0:T(8,128)}, u32[]{:S(2)}) copy-start(f32[256,256]{1,0:T(8,128)} %param.9) | copy-start | bytes 786436
  0.6 5.4 %copy-start.7 = (bf16[1024,1024]{1,0:T(8,128)(2,1)S(1)}, bf16[1024,1024]{1,0:T(8,128)(2,1)}, u32[]{:S(2)}) copy-start(bf16[1024,1024]{1,0:T(8,128)(2,1)} %param.7) | copy-start | bytes 6291460
  6.0 58.3 %copy-start.5 = (f32[1024,256]{1,0:T(8,128)}, f32[1024,256]{1,0:T(8,128)S(1)}, u32[]{:S(2)}) copy-start(f32[1024,256]{1,0:T(8,128)S(1)} %fusion.24) | copy-start | bytes 3145732
  58.5 3.8 %copy-start.11 = (bf16[4,4,4,8,1024]{4,3,2,1,0:T(8,128)(2,1)S(1)}, bf16[4,4,4,8,1024]{4,3,2,1,0:T(8,128)(2,1)}, u32[]{:S(2)}) copy-start(bf16[4,4,4,8,1024]{4,3,2,1,0:T(8,128)(2,1)} %get-tuple-element.11) | copy-start | bytes 3145732
  62.3 3.0 %copy-start.2 = (f32[1024,1000]{0,1:T(8,128)S(1)}, f32[1024,1000]{0,1:T(8,128)}, u32[]{:S(2)}) copy-start(f32[1024,1000]{0,1:T(8,128)} %param.8) | copy-start | bytes 12288004
  74.2 1.7 %copy-start.1 = (f32[640,1024]{1,0:T(8,128)S(1)}, f32[640,1024]{1,0:T(8,128)}, u32[]{:S(2)}) copy-start(f32[640,1024]{1,0:T(8,128)} %copy.17) | copy-start | bytes 7864324
  124.7 1.2 copy-start.10
  124.8 2.7 %copy-start.6 = (f32[1024,256]{1,0:T(8,128)S(1)}, f32[1024,256]{1,0:T(8,128)}, u32[]{:S(2)}) copy-start(f32[1024,256]{1,0:T(8,128)} %copy-done.5) | copy-start | bytes 3145732
  131.0 2.5 %copy-start.8 = (f32[128,1000]{1,0:T(8,128)S(1)}, f32[128,1000]{1,0:T(8,128)}, u32[]{:S(2)}) copy-start(f32[128,1000]{1,0:T(8,128)} %get-tuple-element.8) | copy-start | bytes 1536004
  134.0 3.5 %copy-start.9 = (f32[4,128,1000]{1,2,0:T(8,128)S(1)}, f32[4,128,1000]{1,2,0:T(8,128)}, u32[]{:S(2)}) copy-start(f32[4,128,1000]{1,2,0:T(8,128)} %param.13) | copy-start | bytes 6144004
  135.2 7.0 %copy-start.4 = (f32[1024,512]{1,0:T(8,128)S(1)}, f32[1024,512]{1,0:T(8,128)}, u32[]{:S(2)}) copy-start(f32[1024,512]{1,0:T(8,128)} %fusion.28) | copy-start | bytes 6291460
  137.5 4.8 %copy-start.3 = (f32[1024,1000]{0,1:T(8,128)S(1)}, f32[1024,1000]{0,1:T(8,128)}, u32[]{:S(2)}) copy-start(f32[1024,1000]{0,1:T(8,128)} %param.8) | copy-start | bytes 12288004

commit v2 on v0

v2 whole, which is shorter than its diff:
```python
import functools

import jax
import jax.numpy as jnp
from jax import lax
from jax.experimental import pallas as pl
from jax.experimental.pallas import tpu as pltpu
from jax.sharding import PartitionSpec as P

STEPS = 4
LANES = 128
TILE = 256
MIB = 2**20
SIZES = {"x": 4, "y": 4, "z": 8}

floor_sq = 0.01
length_scale = 0.25
step_size = 0.5

MESH = pl.DeviceIdType.MESH
f32, bf16 = jnp.float32, jnp.bfloat16
NT = (((1,), (1,)), ((), ()))
NN = (((1,), (0,)), ((), ()))


def dot(left, right, dims=NN):
    return lax.dot_general(left, right, dims, preferred_element_type=f32)


def split(value):
    high = value.astype(bf16)
    return high, (value - high.astype(f32)).astype(bf16)


def dot3(left, right, dims=NN):
    return dot(left[0], right[0], dims) + (dot(left[0], right[1], dims) + dot(left[1], right[0], dims))


class Sum:
    def __init__(self, place, theirs, own, out, order, bufs, send, recv):
        sizes, me, device = place
        count = [0]

        def remote(src, dst, to):
            index = count[0]
            count[0] += 1
            return pltpu.make_async_remote_copy(
                src_ref=src,
                dst_ref=dst,
                send_sem=send.at[index],
                recv_sem=recv.at[index],
                device_id=to,
                device_id_type=MESH,
            )

        def columns(index):
            return pl.ds(pl.multiple_of(index * LANES, LANES), LANES)

        def along(ref, dims, axis, index):
            if axis == "z":
                return ref.at[(slice(None),) * (len(dims) + 1) + (columns(index),)]
            return ref.at[tuple(index if dim == axis else slice(None) for dim in dims)]

        def region(fixed):
            return out.at[
                me["x"] if "x" in fixed else slice(None),
                me["y"] if "y" in fixed else slice(None),
                slice(None),
                columns(me["z"]) if "z" in fixed else slice(None),
            ]

        def to(axis, by):
            return lax.rem(me[axis] + by, sizes[axis])

        self.core = remote(theirs, bufs[0], device("c", 1))
        self.stages = []
        copies, terms, dims = [self.core], [own, bufs[0]], "xy"
        for phase in range(3):
            axis = order[phase]
            total, landing = bufs[1 + 2 * phase], bufs[2 + 2 * phase]
            hops = range(1, sizes[axis])
            sends = [
                remote(along(total, dims, axis, to(axis, by)), landing.at[by - 1], device(axis, by))
                for by in hops
            ]
            self.stages.append((copies, terms, total, sends))
            terms = [along(total, dims, axis, me[axis])] + [landing.at[by - 1] for by in hops]
            copies, dims = sends, dims.replace(axis, "")
        total = region("xyz")
        for phase in range(3):
            axis = order[2 - phase]
            here = region(order[: 3 - phase])
            sends = [remote(here, here, device(axis, by)) for by in range(1, sizes[axis])]
            self.stages.append((copies, terms, total, sends))
            copies, terms, total = sends, None, None
        self.back = remote(out, out, device("c", 1))
        self.stages.append((copies, None, None, [self.back]))

    def run(self, stage):
        copies, terms, total, sends = self.stages[stage]
        for copy in copies:
            copy.wait_recv()
        if terms is not None:
            value = terms[0][...]
            for term in terms[1:]:
                value = value + term[...]
            total[...] = value
        for copy in sends:
            copy.start()

    def finish(self):
        for stage in self.stages:
            for copy in stage[3]:
                copy.wait_send()


def sum_scratch(sizes, order, block):
    block = list(block)
    dims = "xy"
    scratch = [pltpu.VMEM(tuple(block), f32)] * 2
    for phase, axis in enumerate(order):
        if axis == "z":
            block[-1] = LANES
        else:
            block.pop(dims.index(axis))
            dims = dims.replace(axis, "")
        scratch.append(pltpu.VMEM((sizes[axis] - 1,) + tuple(block), f32))
        if phase < 2:
            scratch.append(pltpu.VMEM(tuple(block), f32))
    return scratch


ORDERS_X = ("xyz", "yxz")
ORDERS_P = ("xyz", "yxz", "zxy")
BUFS = 7


def main_kernel(
    sizes,
    centers,
    coefs_hbm,
    eigvecs,
    weights,
    landmarks,
    batch_index,
    targets_hbm,
    residual,
    update_high,
    update_low,
    coefs,
    targets,
    right_high,
    right_low,
    center_sq,
    picked,
    arrived,
    points,
    batch,
    kernel,
    batch_sq,
    between,
    predicted,
    gradient,
    predicted_sum,
    gradient_sum,
    effect_high,
    effect_low,
    residual_high,
    residual_low,
    local_sem,
    send_x,
    recv_x,
    send_p,
    recv_p,
    *bufs,
):
    grp, ctr = lax.axis_index("grp"), lax.axis_index("ctr")
    core, y = lax.rem(grp, 2), lax.div(grp, 2)
    z, x = lax.div(ctr, sizes["x"]), lax.rem(ctr, sizes["x"])
    me = {"x": x, "y": y, "z": z}

    def device(axis, by):
        if axis == "c":
            return (y * 2 + 1 - core, ctr)
        to = lax.rem(me[axis] + by, sizes[axis])
        if axis == "x":
            return (grp, z * sizes["x"] + to)
        if axis == "y":
            return (to * 2 + core, ctr)
        return (grp, to * sizes["x"] + x)

    place = (sizes, me, device)
    peers = [("c", 1)] + [(axis, by) for axis in "xyz" for by in range(1, sizes[axis])]
    barrier = pltpu.get_barrier_semaphore()
    for axis, by in peers:
        pl.semaphore_signal(barrier, inc=1, device_id=device(axis, by), device_id_type=MESH)

    count, width = centers.shape
    outputs = coefs_hbm.shape[0]
    eigs = eigvecs.shape[1]
    rows = batch_index.shape[1]
    coefs_in = pltpu.make_async_copy(coefs_hbm, coefs.at[:outputs], local_sem.at[0])
    targets_in = pltpu.make_async_copy(targets_hbm, targets.at[:, :outputs], local_sem.at[1])
    coefs_in.start()
    targets_in.start()
    coefs[outputs:, :] = jnp.zeros((width - outputs, count), f32)
    targets[:, outputs:, :] = jnp.zeros((STEPS, width - outputs, rows), f32)
    pair = 2 * rows
    block = (2,) + tuple(picked.shape[1:])
    row_tile, tile, out_tile = min(TILE, count), min(TILE, width), min(2 * TILE, width)
    offset = (grp * lax.axis_size("ctr") + ctr) * count

    def tiles(length, size):
        def loop(step):
            @pl.loop(0, length // size)
            def _(index):
                step(pl.ds(pl.multiple_of(index * size, size), size))

        return loop

    for step in range(STEPS):
        local = jnp.broadcast_to(batch_index[step : step + 1, :] - offset, (LANES, rows))
        points[step * rows : (step + 1) * rows, :] = local.T

    def is_owned(here, length, start, size):
        local = points[here, 0:1] - start
        return local == lax.broadcasted_iota(jnp.int32, (length, size), 1)

    def pick(index):
        owned = is_owned(pl.ds(pl.multiple_of(index * pair, pair), pair), pair, 0, count)
        owned = jnp.where(owned, 1.0, 0.0).astype(bf16)

        @tiles(width, tile)
        def _(columns):
            value = dot(owned, centers[:, columns])
            picked[pl.ds(index * 2, 2), :, :, :, columns] = value.reshape(block[:-1] + (tile,))

    mine, other = core, 1 - core
    sums_x = [
        Sum(
            place,
            picked.at[other * 2 + k],
            picked.at[mine * 2 + k],
            arrived.at[mine * 2 + k],
            ORDERS_X[k],
            bufs[k * BUFS : (k + 1) * BUFS],
            send_x.at[k],
            recv_x.at[k],
        )
        for k in range(2)
    ]
    pick(other)
    pl.semaphore_wait(barrier, len(peers))
    for part in sums_x:
        part.core.start()
    pick(mine)
    for part in sums_x:
        part.run(0)

    coefs_in.wait()

    @tiles(width, tile // 2)
    def _(here):
        right_high[here, :], right_low[here, :] = split(coefs[here, :])

    for part in sums_x:
        part.run(1)

    eig_high, eig_low = split(eigvecs[...].T)

    @tiles(count, row_tile)
    def _(here):
        local = landmarks[...] - offset - here.start
        at = jnp.where(
            local == lax.broadcasted_iota(jnp.int32, (row_tile, landmarks.shape[1]), 0), 1.0, 0.0
        ).astype(bf16)
        right_high[width:, here] = dot(eig_high, at, NT).astype(bf16)
        right_low[width:, here] = dot(eig_low, at, NT).astype(bf16)

    for part in sums_x:
        part.run(2)
    ones = jnp.ones((8, width), bf16)

    @tiles(count, row_tile)
    def _(here):
        value = centers[here, :].astype(f32)
        high, low = split(value * value)
        center_sq[:, here] = dot(ones, high, NT) + dot(ones, low, NT)

    for stage in range(3, 7):
        for part in sums_x:
            part.run(stage)

    sums_p = [
        Sum(
            place,
            predicted.at[mine * 2 + k],
            predicted.at[other * 2 + k],
            predicted_sum.at[other * 2 + k],
            ORDERS_P[k],
            bufs[(2 + k) * BUFS : (3 + k) * BUFS],
            send_p.at[k],
            recv_p.at[k],
        )
        for k in range(2)
    ]
    sum_g = Sum(
        place, gradient, gradient, gradient_sum, ORDERS_P[2], bufs[4 * BUFS : 5 * BUFS], send_p.at[2], recv_p.at[2]
    )

    def laplace(left_sq, right_sq, inner):
        squared = left_sq + right_sq - 2.0 * inner
        return jnp.exp(jnp.sqrt(jnp.maximum(squared, floor_sq)) * (-1.0 / length_scale))

    def predict(index):
        here = pl.ds(pl.multiple_of(index * pair, pair), pair)
        value = arrived[pl.ds(index * 2, 2)].reshape(pair, width)
        value_sq = jnp.sum(value * value, axis=1, keepdims=True)
        batch_sq[here, :] = jnp.broadcast_to(value_sq, (pair, LANES))
        batch[here, :] = value.astype(bf16)

        @tiles(count, row_tile)
        def _(columns):
            inner = dot(batch[here, :], centers[columns, :], NT)
            high, low = split(laplace(batch_sq[here, 0:1], center_sq[0:1, columns], inner))
            kernel[:pair, columns] = high
            kernel[pair:, columns] = low

        both = dot(kernel[...], right_high[width:, :], NT)
        value = both[:pair] + (both[pair:] + dot(kernel[:pair, :], right_low[width:, :], NT))
        for k in range(2):
            columns = pl.ds(pl.multiple_of((index * 2 + k) * eigs, eigs), eigs)
            gradient[:, :, :, columns] = value[k * rows : (k + 1) * rows].reshape(block[1:-1] + (eigs,))

        @pl.loop(0, width // out_tile)
        def _(step):
            here = pl.ds(pl.multiple_of(step * out_tile, out_tile), out_tile)
            both = dot(right_high[here, :], kernel[...], NT)
            value = both[:, :pair] + (both[:, pair:] + dot(right_low[here, :], kernel[:pair, :], NT))
            for j in range(out_tile // LANES):
                columns = pl.ds(pl.multiple_of(step * out_tile + j * LANES, LANES), LANES)
                for k in range(2):
                    piece = value[j * LANES : (j + 1) * LANES, k * rows : (k + 1) * rows]
                    predicted[index * 2 + k, :, :, :, columns] = piece.reshape(block[1:-1] + (rows,))

    predict(mine)
    for part in sums_p:
        part.core.start()
    for part in sums_x:
        part.back.wait_recv()
    predict(other)
    pl.when(core == 1)(sum_g.core.start)

    def both(stage):
        for part in sums_p:
            part.run(stage)

    def extra(stage):
        pl.when(core == 0)(functools.partial(sum_g.run, stage))

    both(0)
    extra(0)

    total = STEPS * rows
    value = batch[...].astype(f32)
    high, low = split(value * value)
    points_sq = (dot(ones, high, NT) + dot(ones, low, NT))[0:1, :]

    @tiles(total, rows)
    def _(here):
        inner = dot(batch[here, :], batch[...], NT)
        between[here, :] = laplace(batch_sq[here, 0:1], points_sq, inner)

    for stage in range(1, 7):
        both(stage)
        extra(stage)

    pl.when(core == 1)(sum_g.back.wait_recv)
    targets_in.wait()
    projection = gradient_sum[...].reshape(rows, width)
    scale = step_size * weights[...]
    plain, weighted = [], []
    for step in range(STEPS):
        value = projection[:, step * eigs : (step + 1) * eigs]
        plain.append(split(value))
        weighted.append(split(value * scale))
    for step in range(STEPS):
        now = slice(step * rows, (step + 1) * rows)

        @tiles(count, row_tile)
        def _(here, now=now, step=step):
            value = dot3(weighted[step], (right_high[width:, here], right_low[width:, here]))
            value = value - jnp.where(is_owned(now, rows, here.start, row_tile), step_size, 0.0)
            update_high[now, here], update_low[now, here] = split(value)

        for past in range(step):
            then = slice(past * rows, (past + 1) * rows)
            value = dot3(weighted[step], plain[past], NT) - step_size * between[now, then]
            effect_high[now, then], effect_low[now, then] = split(value)
    for part in sums_p:
        part.back.wait_recv()
    for step in range(STEPS):
        now, then = slice(step * rows, (step + 1) * rows), slice(0, step * rows)
        pieces = [
            predicted_sum[step, :, :, :, j * LANES : (j + 1) * LANES].reshape(rows, rows)
            for j in range(width // LANES)
        ]
        value = jnp.concatenate(pieces, axis=0) - targets[step]
        if step > 0:
            value = value + dot3(
                (residual_high[:, then], residual_low[:, then]), (effect_high[now, then], effect_low[now, then]), NT
            )
        residual[step] = value[:outputs]
        if step < STEPS - 1:
            residual_high[:, now], residual_low[:, now] = split(value)

    for part in sums_x + sums_p:
        part.core.wait_send()
        part.finish()
    pl.when(core == 1)(sum_g.core.wait_send)
    pl.when(core == 0)(sum_g.finish)


def update_kernel(update_high, update_low, coefs, residual, new_coefs, residuals):
    residuals[...] = residual[...]
    value = split(jnp.concatenate([residual[step] for step in range(STEPS)], axis=1))
    new_coefs[...] = coefs[...] + dot3(value, (update_high[...], update_low[...]))


def body(sizes, centers, coefs, eigvecs, eig_weights, landmark_index, batch_index, targets):
    count, width = centers.shape
    outputs = coefs.shape[1]
    eigs = eigvecs.shape[1]
    rows = batch_index.shape[1]
    total = STEPS * rows
    block = (sizes["x"], sizes["y"], 8, width)
    copies = 2 + 2 * sum(size - 1 for size in sizes.values())
    bufs = []
    for order in ORDERS_X + ORDERS_P:
        bufs += sum_scratch(sizes, order, block)
    dma = pltpu.SemaphoreType.DMA
    vmem = pl.BlockSpec(memory_space=pltpu.VMEM)
    hbm = pl.BlockSpec(memory_space=pl.ANY)
    residual, update_high, update_low = pl.pallas_call(
        functools.partial(main_kernel, sizes),
        out_shape=[
            jax.ShapeDtypeStruct((STEPS, outputs, rows), f32),
            jax.ShapeDtypeStruct((total, count), bf16),
            jax.ShapeDtypeStruct((total, count), bf16),
        ],
        in_specs=[vmem, hbm, vmem, vmem, vmem, vmem, hbm],
        out_specs=[vmem] * 3,
        scratch_shapes=[
            pltpu.VMEM((width, count), f32),
            pltpu.VMEM((STEPS, width, rows), f32),
            pltpu.VMEM((width + eigs, count), bf16),
            pltpu.VMEM((width + eigs, count), bf16),
            pltpu.VMEM((8, count), f32),
            pltpu.VMEM((STEPS,) + block, f32),
            pltpu.VMEM((STEPS,) + block, f32),
            pltpu.VMEM((total, LANES), jnp.int32),
            pltpu.VMEM((total, width), bf16),
            pltpu.VMEM((4 * rows, count), bf16),
            pltpu.VMEM((total, LANES), f32),
            pltpu.VMEM((total, total), f32),
            pltpu.VMEM((STEPS,) + block, f32),
            pltpu.VMEM(block, f32),
            pltpu.VMEM((STEPS,) + block, f32),
            pltpu.VMEM(block, f32),
            pltpu.VMEM((total, total), bf16),
            pltpu.VMEM((total, total), bf16),
            pltpu.VMEM((width, total), bf16),
            pltpu.VMEM((width, total), bf16),
            dma((2,)),
            dma((2, copies)),
            dma((2, copies)),
            dma((3, copies)),
            dma((3, copies)),
        ]
        + bufs,
        compiler_params=pltpu.CompilerParams(
            collective_id=0, has_side_effects=True, vmem_limit_bytes=56 * MIB
        ),
        name="predict",
    )(
        centers,
        coefs.T,
        eigvecs,
        eig_weights.reshape(1, eigs),
        landmark_index.reshape(1, -1),
        batch_index,
        targets.transpose(0, 2, 1),
    )

    tile = next(tile for tile in (200, 8, outputs) if outputs % tile == 0)
    new_coefs, residuals = pl.pallas_call(
        update_kernel,
        grid=(outputs // tile,),
        out_shape=[
            jax.ShapeDtypeStruct((outputs, count), f32),
            jax.ShapeDtypeStruct((STEPS, outputs, rows), f32),
        ],
        in_specs=[
            pl.BlockSpec((total, count), lambda i: (0, 0)),
            pl.BlockSpec((total, count), lambda i: (0, 0)),
            pl.BlockSpec((tile, count), lambda i: (i, 0)),
            pl.BlockSpec((STEPS, tile, rows), lambda i: (0, i, 0)),
        ],
        out_specs=[
            pl.BlockSpec((tile, count), lambda i: (i, 0)),
            pl.BlockSpec((STEPS, tile, rows), lambda i: (0, i, 0)),
        ],
        compiler_params=pltpu.CompilerParams(vmem_limit_bytes=60 * MIB),
        name="update",
    )(update_high, update_low, coefs.T, residual)
    return new_coefs.T, residuals.transpose(0, 2, 1)


def solution(mesh, sizes=SIZES):
    in_specs = (
        P(("grp", "ctr"), None),
        P(("grp", "ctr"), None),
        P(("grp", "ctr"), None),
        P(),
        P(("grp", "ctr")),
        P(),
        P(),
    )
    out_specs = (P(("grp", "ctr"), None), P())
    return jax.shard_map(
        functools.partial(body, sizes),
        mesh=mesh,
        in_specs=in_specs,
        out_specs=out_specs,
        check_vma=False,
    )
```

time: 2430 us -> 113 us (0.05)
  waiting for transfers between devices: 2240 us -> 0 us
  Pallas kernels: 0 us -> 112 us
  matrix products: 79.5 us -> 0 us
  other arithmetic: 65.1 us -> 0 us
  local copies, waits for them, and re-layouts: 26.1 us -> 0 us
    psum x9 -> x0, waiting for transfers between devices: 2240 us -> none  [the longest x4 989 us: body(): predicted = lax.psum(hdot(kernel, coeffs), ('grp', 'ctr'))]
    pallas_call x0 -> x2, Pallas kernels: none -> 112 us  [the longest x1 103 us: body(): pl.pallas_call(functools.partial(main_kernel, sizes), out_shape=[jax.Shap...]
    dot_general x24 -> x0, matrix products: 79.5 us -> none  [the longest x12 56.6 us: hdot(): jnp.dot(left_mat, right_mat, precision=lax.Precision.HIGHEST, preferred_e...]
    scatter-add x8 -> x0, other arithmetic: 49.9 us -> none  [body(): coeffs = coeffs.at[safe_rows[iteration]].add(batch_update).at[land_local]...]
  transfers between devices with their start and end apart: 9 -> 0, of which waited for: 9 -> 0; matrix products, arithmetic and copies ran while one was open for 2% -> 0% of each run, Pallas kernels for 0% -> 0%
where the time goes in v2:
time: 113 us
  Pallas kernels  112 us (99%)
    pallas_call x1, Pallas kernels, body(): pl.pallas_call(functools.partial(main_kernel, sizes), out_shape=[jax.Shap...  103 us
    pallas_call x1, Pallas kernels, body(): pl.pallas_call(update_kernel, grid=(outputs // tile,), out_shape=[jax.Sha...  9.01 us

profile of v2, /device:TPU:1, one launch (start us, length us, event | category | flops | bytes accessed | tf_op | source)
XLA Modules:
  0.0 112.9 jit_solution(16212674985753132858)
XLA Ops:
  0.6 103.2 %predict.1 = (f32[4,1000,128]{2,1,0:T(8,128)}, bf16[512,1024]{1,0:T(8,128)(2,1)}, bf16[512,1024]{1,0:T(8,128)(2,1)}) custom-call(bf16[1024,1024]{1,0:T(8,128)(2,1)} %centers.1, f32[1000,1024]{1,0:T(8,128)} %bitcast.6, f32[256,256]{1,0:T(8,128)} %eigvecs.1, f32[1,256]{1,0:T(1,128)} %bitcast.9, s32[1,256]{1,0:T(1,128)} %bitcast.10, s32[4,128]{1,0:T(4,128)} %batch_index.1, ...), custom_call_target="tpu_custom_call" | custom-call | tf_op jit(solution)/shard_map/predict/pallas_call | solution.py:444
  103.9 9.0 %update.1 = (f32[1000,1024]{1,0:T(8,128)}, f32[4,1000,128]{2,1,0:T(8,128)}) custom-call(bf16[512,1024]{1,0:T(8,128)(2,1)} %get-tuple-element.7.update_high, bf16[512,1024]{1,0:T(8,128)(2,1)} %get-tuple-element.8.update_low, f32[1000,1024]{1,0:T(8,128)} %bitcast.7, f32[4,1000,128]{2,1,0:T(8,128)} %get-tuple-element.9.residual), custom_call_target="tpu_custom_call" | custom-call | tf_op jit(solution)/shard_map/update/pallas_call | solution.py:496

commit v3 on v2

--- a/solution.py
+++ b/solution.py
@@ -36,29 +36,56 @@
     return dot(left[0], right[0], dims) + (dot(left[0], right[1], dims) + dot(left[1], right[0], dims))
 
 
+def span(index):
+    return pl.ds(pl.multiple_of(index * LANES, LANES), LANES)
+
+
+class Copies:
+    def __init__(self, place, sems, index, like):
+        self.send, self.recv = (sem.at[index] for sem in sems)
+        self.like, self.copies = like, []
+        self.device = place[2]
+
+    def to(self, axis, by, src, dst):
+        self.copies.append(self.copy(axis, by, src, dst))
+
+    def copy(self, axis, by, src, dst):
+        return pltpu.make_async_remote_copy(
+            src_ref=src,
+            dst_ref=dst,
+            send_sem=self.send,
+            recv_sem=self.recv,
+            device_id=self.device(axis, by),
+            device_id_type=MESH,
+        )
+
+    def start(self):
+        for copy in self.copies:
+            copy.start()
+
+    def wait_recv(self):
+        if self.copies:
+            self.copy("c", 1, self.like, self.like).wait_recv()
+
+    def wait_send(self):
+        if self.copies:
+            self.copy("c", 1, self.like, self.like).wait_send()
+
+
+def add(terms, into):
+    value = terms[0][...]
+    for term in terms[1:]:
+        value = value + term[...]
+    into[...] = value
+
+
 class Sum:
-    def __init__(self, place, theirs, own, out, order, bufs, send, recv):
+    def __init__(self, place, theirs, own, out, order, bufs, sems):
         sizes, me, device = place
-        count = [0]
-
-        def remote(src, dst, to):
-            index = count[0]
-            count[0] += 1
-            return pltpu.make_async_remote_copy(
-                src_ref=src,
-                dst_ref=dst,
-                send_sem=send.at[index],
-                recv_sem=recv.at[index],
-                device_id=to,
-                device_id_type=MESH,
-            )
-
-        def columns(index):
-            return pl.ds(pl.multiple_of(index * LANES, LANES), LANES)
 
         def along(ref, dims, axis, index):
             if axis == "z":
-                return ref.at[(slice(None),) * (len(dims) + 1) + (columns(index),)]
+                return ref.at[(slice(None),) * (len(dims) + 1) + (span(index),)]
             return ref.at[tuple(index if dim == axis else slice(None) for dim in dims)]
 
         def region(fixed):
@@ -66,52 +93,167 @@
                 me["x"] if "x" in fixed else slice(None),
                 me["y"] if "y" in fixed else slice(None),
                 slice(None),
-                columns(me["z"]) if "z" in fixed else slice(None),
+                span(me["z"]) if "z" in fixed else slice(None),
             ]
 
-        def to(axis, by):
-            return lax.rem(me[axis] + by, sizes[axis])
-
-        self.core = remote(theirs, bufs[0], device("c", 1))
+        self.core = Copies(place, sems, 0, bufs[0])
+        self.core.to("c", 1, theirs, bufs[0])
         self.stages = []
-        copies, terms, dims = [self.core], [own, bufs[0]], "xy"
+        copies, terms, dims = self.core, [own, bufs[0]], "xy"
         for phase in range(3):
             axis = order[phase]
             total, landing = bufs[1 + 2 * phase], bufs[2 + 2 * phase]
-            hops = range(1, sizes[axis])
-            sends = [
-                remote(along(total, dims, axis, to(axis, by)), landing.at[by - 1], device(axis, by))
-                for by in hops
-            ]
+            sends = Copies(place, sems, 1 + phase, landing)
+            for by in range(1, sizes[axis]):
+                index = lax.rem(me[axis] + by, sizes[axis])
+                sends.to(axis, by, along(total, dims, axis, index), landing.at[by - 1])
             self.stages.append((copies, terms, total, sends))
-            terms = [along(total, dims, axis, me[axis])] + [landing.at[by - 1] for by in hops]
+            terms = [along(total, dims, axis, me[axis])] + [landing.at[by - 1] for by in range(1, sizes[axis])]
             copies, dims = sends, dims.replace(axis, "")
         total = region("xyz")
         for phase in range(3):
             axis = order[2 - phase]
             here = region(order[: 3 - phase])
-            sends = [remote(here, here, device(axis, by)) for by in range(1, sizes[axis])]
+            sends = Copies(place, sems, 4 + phase, bufs[6 - 2 * phase])
+            for by in range(1, sizes[axis]):
+                sends.to(axis, by, here, here)
             self.stages.append((copies, terms, total, sends))
             copies, terms, total = sends, None, None
-        self.back = remote(out, out, device("c", 1))
-        self.stages.append((copies, None, None, [self.back]))
+        self.back = Copies(place, sems, 7, bufs[0])
+        self.back.to("c", 1, out, out)
+        self.stages.append((copies, None, None, self.back))
 
     def run(self, stage):
         copies, terms, total, sends = self.stages[stage]
-        for copy in copies:
-            copy.wait_recv()
+        copies.wait_recv()
         if terms is not None:
-            value = terms[0][...]
-            for term in terms[1:]:
-                value = value + term[...]
-            total[...] = value
-        for copy in sends:
-            copy.start()
+            add(terms, total)
+        sends.start()
 
     def finish(self):
         for stage in self.stages:
-            for copy in stage[3]:
-                copy.wait_send()
+            stage[3].wait_send()
+
+
+class Pair:
+    def __init__(self, place, theirs, own, out, bufs, sems):
+        sizes, me, device = place
+        self.taken, self.total0, landing0, self.total1, landing1, self.total2, landing2 = bufs
+        self.far = sorted(range(sizes["x"]), key=lambda by: -min(by, sizes["x"] - by))
+
+        def first(ref, k, index):
+            return ref.at[k, index] if k == 0 else ref.at[k, :, index]
+
+        def to(axis, by):
+            return lax.rem(me[axis] + by, sizes[axis])
+
+        self.core, self.one, self.two, self.up2, self.up1, self.back = [], [], [], [], [], []
+        self.terms1, self.terms2, self.sums = [], [], []
+        for k in range(2):
+            axis, other = ("x", "y") if k == 0 else ("y", "x")
+            base, side = 11 * k, sizes[axis]
+            core, up1 = {}, {}
+            one = Copies(place, sems, base + 1, landing0.at[k])
+            two = Copies(place, sems, base + 2, landing1.at[k])
+            up2 = Copies(place, sems, base + 3, landing1.at[k])
+            back = Copies(place, sems, base, self.taken.at[k])
+            for by in range(side):
+                core[by] = Copies(place, sems, base + 4 + by, landing0.at[k, 0])
+                index = to(axis, by)
+                core[by].to("c", 1, first(theirs, k, index), first(self.taken, k, index))
+                here = first(out, k, index)
+                back.to("c", 1, here, here)
+            here = out.at[k, me["x"], me["y"]]
+            for by in range(1, sizes[other]):
+                two.to(other, by, self.total1.at[k, to(other, by)], landing1.at[k, by - 1])
+                up2.to(other, by, here, here)
+            here = first(out, k, me[axis])
+            for by in range(1, sizes[axis]):
+                one.to(axis, by, first(self.total0, k, to(axis, by)), landing0.at[k, by - 1])
+                up1[by] = Copies(place, sems, base + 7 + by, landing0.at[k, 0])
+                up1[by].to(axis, by, here, here)
+            self.sums.append(
+                [
+                    [first(ref, k, to(axis, by)) for ref in (own, self.taken, self.total0)]
+                    for by in range(side)
+                ]
+            )
+            self.terms1.append(
+                [first(self.total0, k, me[axis])] + [landing0.at[k, by - 1] for by in range(1, sizes[axis])]
+            )
+            self.terms2.append(
+                [self.total1.at[k, me[other]]] + [landing1.at[k, by - 1] for by in range(1, sizes[other])]
+            )
+            self.core.append(core)
+            self.one.append(one)
+            self.two.append(two)
+            self.up2.append(up2)
+            self.up1.append(up1)
+            self.back.append(back)
+        self.down = Copies(place, sems, 22, landing2)
+        self.up = Copies(place, sems, 23, landing2)
+        self.mine = out.at[:, me["x"], me["y"], :, span(me["z"])]
+        for by in range(1, sizes["z"]):
+            self.down.to("z", by, self.total2.at[:, :, span(to("z", by))], landing2.at[by - 1])
+            self.up.to("z", by, self.mine, self.mine)
+        self.last = [self.total2.at[:, :, span(me["z"])]] + [landing2.at[by - 1] for by in range(1, sizes["z"])]
+
+    def start_core(self):
+        for by in self.far:
+            for k in range(2):
+                self.core[k][by].start()
+
+    def run(self, stage):
+        if stage == 0:
+            for by in self.far:
+                for k in range(2):
+                    self.core[k][by].wait_recv()
+                    own, taken, total = self.sums[k][by]
+                    add([own, taken], total)
+                    if by > 0:
+                        self.one[k].copies[by - 1].start()
+        if stage == 6:
+            for by in reversed(self.far[:-1]):
+                for k in range(2):
+                    self.up1[k][by].wait_recv()
+                    self.back[k].copies[len(self.far) - by].start()
+        if stage == 3:
+            self.down.wait_recv()
+            add(self.last, self.mine)
+            self.up.start()
+        elif stage == 4:
+            self.up.wait_recv()
+        for k in range(2):
+            if stage == 1:
+                self.one[k].wait_recv()
+                add(self.terms1[k], self.total1.at[k])
+                self.two[k].start()
+            elif stage == 2:
+                self.two[k].wait_recv()
+                add(self.terms2[k], self.total2.at[k])
+            elif stage == 4:
+                self.up2[k].start()
+            elif stage == 5:
+                self.up2[k].wait_recv()
+                for by in self.far[:-1]:
+                    self.up1[k][by].start()
+                self.back[k].copies[0].start()
+        if stage == 2:
+            self.down.start()
+
+    def finish(self):
+        for core in self.core:
+            for copies in core.values():
+                copies.wait_send()
+        for copies in self.one + self.two + [self.down, self.up] + self.up2:
+            copies.wait_send()
+
+    def finish_last(self):
+        for up1 in self.up1:
+            for copies in up1.values():
+                copies.wait_send()
+        for copies in self.back:
+            copies.wait_send()
 
 
 def sum_scratch(sizes, order, block):
@@ -130,8 +272,21 @@
     return scratch
 
 
-ORDERS_X = ("xyz", "yxz")
-ORDERS_P = ("xyz", "yxz", "zxy")
+def pair_scratch(sizes, block):
+    side, deep, rows, width = block
+    shapes = [
+        (2,) + block,
+        (2,) + block,
+        (2, side - 1, side, rows, width),
+        (2, side, rows, width),
+        (2, side - 1, rows, width),
+        (2, rows, width),
+        (sizes["z"] - 1, 2, rows, LANES),
+    ]
+    return [pltpu.VMEM(shape, f32) for shape in shapes]
+
+
+EXTRA = "zxy"
 BUFS = 7
 
 
@@ -172,6 +327,8 @@
     recv_x,
     send_p,
     recv_p,
+    send_g,
+    recv_g,
     *bufs,
 ):
     grp, ctr = lax.axis_index("grp"), lax.axis_index("ctr")
@@ -207,7 +364,7 @@
     targets[:, outputs:, :] = jnp.zeros((STEPS, width - outputs, rows), f32)
     pair = 2 * rows
     block = (2,) + tuple(picked.shape[1:])
-    row_tile, tile, out_tile = min(TILE, count), min(TILE, width), min(2 * TILE, width)
+    row_tile, tile, out_tile = min(TILE, count), min(TILE, width), max(width // 2, LANES)
     offset = (grp * lax.axis_size("ctr") + ctr) * count
 
     def tiles(length, size):
@@ -236,26 +393,15 @@
             picked[pl.ds(index * 2, 2), :, :, :, columns] = value.reshape(block[:-1] + (tile,))
 
     mine, other = core, 1 - core
-    sums_x = [
-        Sum(
-            place,
-            picked.at[other * 2 + k],
-            picked.at[mine * 2 + k],
-            arrived.at[mine * 2 + k],
-            ORDERS_X[k],
-            bufs[k * BUFS : (k + 1) * BUFS],
-            send_x.at[k],
-            recv_x.at[k],
-        )
-        for k in range(2)
-    ]
+    def two(ref, index):
+        return ref.at[pl.ds(index * 2, 2)]
+
+    sum_x = Pair(place, two(picked, other), two(picked, mine), two(arrived, mine), bufs[:BUFS], (send_x, recv_x))
     pick(other)
     pl.semaphore_wait(barrier, len(peers))
-    for part in sums_x:
-        part.core.start()
+    sum_x.start_core()
     pick(mine)
-    for part in sums_x:
-        part.run(0)
+    sum_x.run(0)
 
     coefs_in.wait()
 
@@ -263,8 +409,7 @@
     def _(here):
         right_high[here, :], right_low[here, :] = split(coefs[here, :])
 
-    for part in sums_x:
-        part.run(1)
+    sum_x.run(1)
 
     eig_high, eig_low = split(eigvecs[...].T)
 
@@ -277,8 +422,7 @@
         right_high[width:, here] = dot(eig_high, at, NT).astype(bf16)
         right_low[width:, here] = dot(eig_low, at, NT).astype(bf16)
 
-    for part in sums_x:
-        part.run(2)
+    sum_x.run(2)
     ones = jnp.ones((8, width), bf16)
 
     @tiles(count, row_tile)
@@ -288,31 +432,23 @@
         center_sq[:, here] = dot(ones, high, NT) + dot(ones, low, NT)
 
     for stage in range(3, 7):
-        for part in sums_x:
-            part.run(stage)
-
-    sums_p = [
-        Sum(
-            place,
-            predicted.at[mine * 2 + k],
-            predicted.at[other * 2 + k],
-            predicted_sum.at[other * 2 + k],
-            ORDERS_P[k],
-            bufs[(2 + k) * BUFS : (3 + k) * BUFS],
-            send_p.at[k],
-            recv_p.at[k],
-        )
-        for k in range(2)
-    ]
-    sum_g = Sum(
-        place, gradient, gradient, gradient_sum, ORDERS_P[2], bufs[4 * BUFS : 5 * BUFS], send_p.at[2], recv_p.at[2]
+        sum_x.run(stage)
+
+    sum_p = Pair(
+        place,
+        two(predicted, mine),
+        two(predicted, other),
+        two(predicted_sum, other),
+        bufs[BUFS : 2 * BUFS],
+        (send_p, recv_p),
     )
+    sum_g = Sum(place, gradient, gradient, gradient_sum, EXTRA, bufs[2 * BUFS :], (send_g, recv_g))
 
     def laplace(left_sq, right_sq, inner):
         squared = left_sq + right_sq - 2.0 * inner
         return jnp.exp(jnp.sqrt(jnp.maximum(squared, floor_sq)) * (-1.0 / length_scale))
 
-    def predict(index):
+    def predict(index, between_them):
         here = pl.ds(pl.multiple_of(index * pair, pair), pair)
         value = arrived[pl.ds(index * 2, 2)].reshape(pair, width)
         value_sq = jnp.sum(value * value, axis=1, keepdims=True)
@@ -332,34 +468,32 @@
             columns = pl.ds(pl.multiple_of((index * 2 + k) * eigs, eigs), eigs)
             gradient[:, :, :, columns] = value[k * rows : (k + 1) * rows].reshape(block[1:-1] + (eigs,))
 
-        @pl.loop(0, width // out_tile)
-        def _(step):
-            here = pl.ds(pl.multiple_of(step * out_tile, out_tile), out_tile)
+        between_them()
+        for step in range(width // out_tile):
+            here = slice(step * out_tile, (step + 1) * out_tile)
             both = dot(right_high[here, :], kernel[...], NT)
             value = both[:, :pair] + (both[:, pair:] + dot(right_low[here, :], kernel[:pair, :], NT))
             for j in range(out_tile // LANES):
-                columns = pl.ds(pl.multiple_of(step * out_tile + j * LANES, LANES), LANES)
+                columns = slice(step * out_tile + j * LANES, step * out_tile + (j + 1) * LANES)
                 for k in range(2):
                     piece = value[j * LANES : (j + 1) * LANES, k * rows : (k + 1) * rows]
                     predicted[index * 2 + k, :, :, :, columns] = piece.reshape(block[1:-1] + (rows,))
 
-    predict(mine)
-    for part in sums_p:
-        part.core.start()
-    for part in sums_x:
-        part.back.wait_recv()
-    predict(other)
-    pl.when(core == 1)(sum_g.core.start)
-
-    def both(stage):
-        for part in sums_p:
-            part.run(stage)
+    def send_extra():
+        pl.when(core == 1)(sum_g.core.start)
 
     def extra(stage):
         pl.when(core == 0)(functools.partial(sum_g.run, stage))
 
-    both(0)
+    predict(mine, lambda: None)
+    sum_p.start_core()
+    for k in range(2):
+        sum_x.back[k].wait_recv()
+    predict(other, send_extra)
+    sum_p.run(0)
     extra(0)
+    sum_x.finish()
+    sum_x.finish_last()
 
     total = STEPS * rows
     value = batch[...].astype(f32)
@@ -372,7 +506,7 @@
         between[here, :] = laplace(batch_sq[here, 0:1], points_sq, inner)
 
     for stage in range(1, 7):
-        both(stage)
+        sum_p.run(stage)
         extra(stage)
 
     pl.when(core == 1)(sum_g.back.wait_recv)
@@ -397,8 +531,9 @@
             then = slice(past * rows, (past + 1) * rows)
             value = dot3(weighted[step], plain[past], NT) - step_size * between[now, then]
             effect_high[now, then], effect_low[now, then] = split(value)
-    for part in sums_p:
-        part.back.wait_recv()
+    sum_p.finish()
+    for k in range(2):
+        sum_p.back[k].wait_recv()
     for step in range(STEPS):
         now, then = slice(step * rows, (step + 1) * rows), slice(0, step * rows)
         pieces = [
@@ -414,17 +549,20 @@
         if step < STEPS - 1:
             residual_high[:, now], residual_low[:, now] = split(value)
 
-    for part in sums_x + sums_p:
-        part.core.wait_send()
-        part.finish()
+    sum_p.finish_last()
     pl.when(core == 1)(sum_g.core.wait_send)
     pl.when(core == 0)(sum_g.finish)
 
 
-def update_kernel(update_high, update_low, coefs, residual, new_coefs, residuals):
-    residuals[...] = residual[...]
-    value = split(jnp.concatenate([residual[step] for step in range(STEPS)], axis=1))
-    new_coefs[...] = coefs[...] + dot3(value, (update_high[...], update_low[...]))
+def update_kernel(update_high, update_low, coefs, residual, new_coefs, residuals, high, low):
+    step = pl.program_id(0)
+
+    @pl.when(step == 0)
+    def _():
+        high[...], low[...] = split(jnp.concatenate([residual[step] for step in range(STEPS)], axis=1))
+
+    residuals[0] = residual[step]
+    new_coefs[...] = coefs[...] + dot3((high[...], low[...]), (update_high[...], update_low[...]))
 
 
 def body(sizes, centers, coefs, eigvecs, eig_weights, landmark_index, batch_index, targets):
@@ -434,10 +572,7 @@
     rows = batch_index.shape[1]
     total = STEPS * rows
     block = (sizes["x"], sizes["y"], 8, width)
-    copies = 2 + 2 * sum(size - 1 for size in sizes.values())
-    bufs = []
-    for order in ORDERS_X + ORDERS_P:
-        bufs += sum_scratch(sizes, order, block)
+    bufs = pair_scratch(sizes, block) * 2 + sum_scratch(sizes, EXTRA, block)
     dma = pltpu.SemaphoreType.DMA
     vmem = pl.BlockSpec(memory_space=pltpu.VMEM)
     hbm = pl.BlockSpec(memory_space=pl.ANY)
@@ -472,10 +607,12 @@
             pltpu.VMEM((width, total), bf16),
             pltpu.VMEM((width, total), bf16),
             dma((2,)),
-            dma((2, copies)),
-            dma((2, copies)),
-            dma((3, copies)),
-            dma((3, copies)),
+            dma((24,)),
+            dma((24,)),
+            dma((24,)),
+            dma((24,)),
+            dma((8,)),
+            dma((8,)),
         ]
         + bufs,
         compiler_params=pltpu.CompilerParams(
@@ -492,24 +629,25 @@
         targets.transpose(0, 2, 1),
     )
 
-    tile = next(tile for tile in (200, 8, outputs) if outputs % tile == 0)
+    tile = count // STEPS
     new_coefs, residuals = pl.pallas_call(
         update_kernel,
-        grid=(outputs // tile,),
+        grid=(STEPS,),
         out_shape=[
             jax.ShapeDtypeStruct((outputs, count), f32),
             jax.ShapeDtypeStruct((STEPS, outputs, rows), f32),
         ],
         in_specs=[
-            pl.BlockSpec((total, count), lambda i: (0, 0)),
-            pl.BlockSpec((total, count), lambda i: (0, 0)),
-            pl.BlockSpec((tile, count), lambda i: (i, 0)),
-            pl.BlockSpec((STEPS, tile, rows), lambda i: (0, i, 0)),
+            pl.BlockSpec((total, tile), lambda i: (0, i)),
+            pl.BlockSpec((total, tile), lambda i: (0, i)),
+            pl.BlockSpec((outputs, tile), lambda i: (0, i)),
+            pl.BlockSpec((STEPS, outputs, rows), lambda i: (0, 0, 0)),
         ],
         out_specs=[
-            pl.BlockSpec((tile, count), lambda i: (i, 0)),
-            pl.BlockSpec((STEPS, tile, rows), lambda i: (0, i, 0)),
+            pl.BlockSpec((outputs, tile), lambda i: (0, i)),
+            pl.BlockSpec((1, outputs, rows), lambda i: (i, 0, 0)),
         ],
+        scratch_shapes=[pltpu.VMEM((outputs, total), bf16)] * 2,
         compiler_params=pltpu.CompilerParams(vmem_limit_bytes=60 * MIB),
         name="update",
     )(update_high, update_low, coefs.T, residual)

time: 113 us -> 113 us (level)
  no operation moved by 1% of the time
where the time goes in v3:
time: 113 us
  Pallas kernels  113 us (100%)
    pallas_call x1, Pallas kernels, body(): pl.pallas_call(functools.partial(main_kernel, sizes), out_shape=[jax.Shap...  104 us
    pallas_call x1, Pallas kernels, body(): pl.pallas_call(update_kernel, grid=(STEPS,), out_shape=[jax.ShapeDtypeStr...  8.59 us

profile of v3, /device:TPU:1, one launch (start us, length us, event | category | flops | bytes accessed | tf_op | source)
XLA Modules:
  0.0 113.2 jit_solution(2114517346777429258)
XLA Ops:
  0.6 103.9 %predict.1 = (f32[4,1000,128]{2,1,0:T(8,128)}, bf16[512,1024]{1,0:T(8,128)(2,1)}, bf16[512,1024]{1,0:T(8,128)(2,1)}) custom-call(bf16[1024,1024]{1,0:T(8,128)(2,1)} %centers.1, f32[1000,1024]{1,0:T(8,128)} %bitcast.6, f32[256,256]{1,0:T(8,128)} %eigvecs.1, f32[1,256]{1,0:T(1,128)} %bitcast.9, s32[1,256]{1,0:T(1,128)} %bitcast.10, s32[4,128]{1,0:T(4,128)} %batch_index.1, ...), custom_call_target="tpu_custom_call" | custom-call | tf_op jit(solution)/shard_map/predict/pallas_call | solution.py:579
  104.6 8.6 %update.1 = (f32[1000,1024]{1,0:T(8,128)}, f32[4,1000,128]{2,1,0:T(8,128)}) custom-call(bf16[512,1024]{1,0:T(8,128)(2,1)} %get-tuple-element.7.update_high, bf16[512,1024]{1,0:T(8,128)(2,1)} %get-tuple-element.8.update_low, f32[1000,1024]{1,0:T(8,128)} %bitcast.7, f32[4,1000,128]{2,1,0:T(8,128)} %get-tuple-element.9.residual), custom_call_target="tpu_custom_call" | custom-call | tf_op jit(solution)/shard_map/update/pallas_call | solution.py:633

commit v4 on v3

--- a/solution.py
+++ b/solution.py
@@ -292,13 +292,18 @@
 
 def main_kernel(
     sizes,
-    centers,
+    centers_hbm,
     coefs_hbm,
-    eigvecs,
+    eigvecs_hbm,
     weights,
     landmarks,
     batch_index,
     targets_hbm,
+    residual_hbm,
+    update_high_hbm,
+    update_low_hbm,
+    centers,
+    eigvecs,
     residual,
     update_high,
     update_low,
@@ -358,7 +363,19 @@
     rows = batch_index.shape[1]
     coefs_in = pltpu.make_async_copy(coefs_hbm, coefs.at[:outputs], local_sem.at[0])
     targets_in = pltpu.make_async_copy(targets_hbm, targets.at[:, :outputs], local_sem.at[1])
+    centers_in = pltpu.make_async_copy(centers_hbm, centers, local_sem.at[2])
+    eigvecs_in = pltpu.make_async_copy(eigvecs_hbm, eigvecs, local_sem.at[3])
+    updates_out = [
+        pltpu.make_async_copy(update_high, update_high_hbm, local_sem.at[4]),
+        pltpu.make_async_copy(update_low, update_low_hbm, local_sem.at[5]),
+    ]
+    residuals_out = [
+        pltpu.make_async_copy(residual.at[step], residual_hbm.at[step], local_sem.at[6 + step])
+        for step in range(STEPS)
+    ]
+    centers_in.start()
     coefs_in.start()
+    eigvecs_in.start()
     targets_in.start()
     coefs[outputs:, :] = jnp.zeros((width - outputs, count), f32)
     targets[:, outputs:, :] = jnp.zeros((STEPS, width - outputs, rows), f32)
@@ -397,6 +414,7 @@
         return ref.at[pl.ds(index * 2, 2)]
 
     sum_x = Pair(place, two(picked, other), two(picked, mine), two(arrived, mine), bufs[:BUFS], (send_x, recv_x))
+    centers_in.wait()
     pick(other)
     pl.semaphore_wait(barrier, len(peers))
     sum_x.start_core()
@@ -411,6 +429,7 @@
 
     sum_x.run(1)
 
+    eigvecs_in.wait()
     eig_high, eig_low = split(eigvecs[...].T)
 
     @tiles(count, row_tile)
@@ -531,6 +550,8 @@
             then = slice(past * rows, (past + 1) * rows)
             value = dot3(weighted[step], plain[past], NT) - step_size * between[now, then]
             effect_high[now, then], effect_low[now, then] = split(value)
+    for copy in updates_out:
+        copy.start()
     sum_p.finish()
     for k in range(2):
         sum_p.back[k].wait_recv()
@@ -546,10 +567,13 @@
                 (residual_high[:, then], residual_low[:, then]), (effect_high[now, then], effect_low[now, then]), NT
             )
         residual[step] = value[:outputs]
+        residuals_out[step].start()
         if step < STEPS - 1:
             residual_high[:, now], residual_low[:, now] = split(value)
 
     sum_p.finish_last()
+    for copy in updates_out + residuals_out:
+        copy.wait()
     pl.when(core == 1)(sum_g.core.wait_send)
     pl.when(core == 0)(sum_g.finish)
 
@@ -583,9 +607,14 @@
             jax.ShapeDtypeStruct((total, count), bf16),
             jax.ShapeDtypeStruct((total, count), bf16),
         ],
-        in_specs=[vmem, hbm, vmem, vmem, vmem, vmem, hbm],
-        out_specs=[vmem] * 3,
+        in_specs=[hbm, hbm, hbm, vmem, vmem, vmem, hbm],
+        out_specs=[hbm] * 3,
         scratch_shapes=[
+            pltpu.VMEM((count, width), bf16),
+            pltpu.VMEM(eigvecs.shape, f32),
+            pltpu.VMEM((STEPS, outputs, rows), f32),
+            pltpu.VMEM((total, count), bf16),
+            pltpu.VMEM((total, count), bf16),
             pltpu.VMEM((width, count), f32),
             pltpu.VMEM((STEPS, width, rows), f32),
             pltpu.VMEM((width + eigs, count), bf16),
@@ -606,7 +635,7 @@
             pltpu.VMEM((total, total), bf16),
             pltpu.VMEM((width, total), bf16),
             pltpu.VMEM((width, total), bf16),
-            dma((2,)),
+            dma((6 + STEPS,)),
             dma((24,)),
             dma((24,)),
             dma((24,)),

time: 113 us -> 109 us (0.965)
  Pallas kernels: 113 us -> 109 us
    pallas_call x1, Pallas kernels: 104 us -> 100 us  [body(): pl.pallas_call(functools.partial(main_kernel, sizes), out_shape=[jax.Shap...]
where the time goes in v4:
time: 109 us
  Pallas kernels  109 us (100%)
    pallas_call x1, Pallas kernels, body(): pl.pallas_call(functools.partial(main_kernel, sizes), out_shape=[jax.Shap...  100 us
    pallas_call x1, Pallas kernels, body(): pl.pallas_call(update_kernel, grid=(STEPS,), out_shape=[jax.ShapeDtypeStr...  8.59 us

profile of v4, /device:TPU:1, one launch (start us, length us, event | category | flops | bytes accessed | tf_op | source)
XLA Modules:
  0.0 109.2 jit_solution(4534780515580034820)
XLA Ops:
  0.6 100.0 %predict.1 = (f32[4,1000,128]{2,1,0:T(8,128)}, bf16[512,1024]{1,0:T(8,128)(2,1)}, bf16[512,1024]{1,0:T(8,128)(2,1)}) custom-call(bf16[1024,1024]{1,0:T(8,128)(2,1)} %centers_hbm.1, f32[1000,1024]{1,0:T(8,128)} %bitcast.6, f32[256,256]{1,0:T(8,128)} %eigvecs_hbm.1, f32[1,256]{1,0:T(1,128)} %bitcast.9, s32[1,256]{1,0:T(1,128)} %bitcast.10, ...), custom_call_target="tpu_custom_call" | custom-call | tf_op jit(solution)/shard_map/predict/pallas_call | solution.py:603
  100.6 8.6 %update.1 = (f32[1000,1024]{1,0:T(8,128)}, f32[4,1000,128]{2,1,0:T(8,128)}) custom-call(bf16[512,1024]{1,0:T(8,128)(2,1)} %get-tuple-element.7.update_high, bf16[512,1024]{1,0:T(8,128)(2,1)} %get-tuple-element.8.update_low, f32[1000,1024]{1,0:T(8,128)} %bitcast.7, f32[4,1000,128]{2,1,0:T(8,128)} %get-tuple-element.9.residual), custom_call_target="tpu_custom_call" | custom-call | tf_op jit(solution)/shard_map/update/pallas_call | solution.py:662

commit v5 on v4

--- a/solution.py
+++ b/solution.py
@@ -537,19 +537,20 @@
         value = projection[:, step * eigs : (step + 1) * eigs]
         plain.append(split(value))
         weighted.append(split(value * scale))
-    for step in range(STEPS):
-        now = slice(step * rows, (step + 1) * rows)
-
-        @tiles(count, row_tile)
-        def _(here, now=now, step=step):
-            value = dot3(weighted[step], (right_high[width:, here], right_low[width:, here]))
-            value = value - jnp.where(is_owned(now, rows, here.start, row_tile), step_size, 0.0)
-            update_high[now, here], update_low[now, here] = split(value)
-
-        for past in range(step):
-            then = slice(past * rows, (past + 1) * rows)
-            value = dot3(weighted[step], plain[past], NT) - step_size * between[now, then]
-            effect_high[now, then], effect_low[now, then] = split(value)
+    weighted_all = tuple(jnp.concatenate([value[i] for value in weighted], axis=0) for i in range(2))
+    plain_all = tuple(jnp.concatenate([value[i] for value in plain], axis=0) for i in range(2))
+
+    @tiles(count, row_tile)
+    def _(here):
+        value = dot3(weighted_all, (right_high[width:, here], right_low[width:, here]))
+        value = value - jnp.where(is_owned(slice(0, total), total, here.start, row_tile), step_size, 0.0)
+        update_high[:, here], update_low[:, here] = split(value)
+
+    for step in range(1, STEPS):
+        now, then = slice(step * rows, (step + 1) * rows), slice(0, step * rows)
+        past = tuple(value[: step * rows] for value in plain_all)
+        value = dot3(weighted[step], past, NT) - step_size * between[now, then]
+        effect_high[now, then], effect_low[now, then] = split(value)
     for copy in updates_out:
         copy.start()
     sum_p.finish()

time: 109 us -> 107 us (0.982)
  Pallas kernels: 109 us -> 106 us
    pallas_call x1, Pallas kernels: 100 us -> 97.4 us  [body(): pl.pallas_call(functools.partial(main_kernel, sizes), out_shape=[jax.Shap...]
where the time goes in v5:
time: 107 us
  Pallas kernels  106 us (99%)
    pallas_call x1, Pallas kernels, body(): pl.pallas_call(functools.partial(main_kernel, sizes), out_shape=[jax.Shap...  97.4 us
    pallas_call x1, Pallas kernels, body(): pl.pallas_call(update_kernel, grid=(STEPS,), out_shape=[jax.ShapeDtypeStr...  8.59 us

profile of v5, /device:TPU:1, one launch (start us, length us, event | category | flops | bytes accessed | tf_op | source)
XLA Modules:
  0.0 106.6 jit_solution(8951084674677867150)
XLA Ops:
  0.6 97.4 %predict.1 = (f32[4,1000,128]{2,1,0:T(8,128)}, bf16[512,1024]{1,0:T(8,128)(2,1)}, bf16[512,1024]{1,0:T(8,128)(2,1)}) custom-call(bf16[1024,1024]{1,0:T(8,128)(2,1)} %centers_hbm.1, f32[1000,1024]{1,0:T(8,128)} %bitcast.6, f32[256,256]{1,0:T(8,128)} %eigvecs_hbm.1, f32[1,256]{1,0:T(1,128)} %bitcast.9, s32[1,256]{1,0:T(1,128)} %bitcast.10, ...), custom_call_target="tpu_custom_call" | custom-call | tf_op jit(solution)/shard_map/predict/pallas_call | solution.py:604
  98.0 8.6 %update.1 = (f32[1000,1024]{1,0:T(8,128)}, f32[4,1000,128]{2,1,0:T(8,128)}) custom-call(bf16[512,1024]{1,0:T(8,128)(2,1)} %get-tuple-element.7.update_high, bf16[512,1024]{1,0:T(8,128)(2,1)} %get-tuple-element.8.update_low, f32[1000,1024]{1,0:T(8,128)} %bitcast.7, f32[4,1000,128]{2,1,0:T(8,128)} %get-tuple-element.9.residual), custom_call_target="tpu_custom_call" | custom-call | tf_op jit(solution)/shard_map/update/pallas_call | solution.py:663
